TPU v7x, 32 devices: a whole 2x2x4 slice. The times are simulated.
32 devices in a mesh: ctx: 8 (over z, x), ch: 4 (over y, core).
Axes of the slice: x: 2, y: 2, z: 4, core: 2. Of those that a mesh axis runs over, the one named last changes fastest.
Arguments:
- query_gate: bfloat16 [4096, 4096], P('ctx', 'ch'), may hold values from -6 to 6
- key_gate: bfloat16 [4096, 4096], P('ctx', 'ch'), may hold values from -6 to 6
- value_in: bfloat16 [4096, 4096], P('ctx', 'ch'), may hold values from -6 to 6
- filter_taps: float32 [4096, 4096], P(None, 'ch'), may hold values from -0.09375 to 0.09375
- skip_gain: float32 [4096], P('ch'), may hold values from -4 to 4
- out_weight: bfloat16 [4096, 4096], P('ch'), may hold values from -0.09375 to 0.09375
Outputs:
- mixed_out: bfloat16 [4096, 4096], P('ctx', 'ch')
All inputs are finite; a program needn't handle non-finite values.
Results may differ from a plain program's by a relative error of at most 0.017.
Values may be sent and summed in bfloat16 or wider, within the bound.
A program may use at most 192 MiB of HBM per device.

v0:
```python
import ml_dtypes
import numpy as np

import jax
import jax.numpy as jnp
from jax import lax
from jax.sharding import PartitionSpec as P

BF16 = jnp.bfloat16
F32 = jnp.float32


def transform_tables(length):
    freqs = np.concatenate([np.arange(0, length, 2), np.arange(1, length, 2)])[:, None]
    times = np.arange(length)[None, :]
    angle = (freqs * times % (2 * length)) * (np.pi / length)
    real, imag = np.cos(angle), -np.sin(angle)
    imag[0] = 1.0 - 2.0 * (np.arange(length) % 2)
    forward = np.concatenate([real, imag], axis=0)
    angle = (freqs * (times + length) % (2 * length)) * (np.pi / length)
    real, imag = np.cos(angle) / length, -np.sin(angle) / length
    real[0] = 0.5 / length
    imag[0] = (1.0 - 2.0 * ((np.arange(length) + length) % 2)) * 0.5 / length
    inverse = np.concatenate([real, imag], axis=0).T
    return forward.astype(ml_dtypes.bfloat16), inverse.astype(ml_dtypes.bfloat16)


def long_conv(x, taps, forward, inverse):
    spans, length, _ = x.shape
    win = taps.shape[0]
    data = jnp.einsum("mn,knc->kmc", forward, x, preferred_element_type=F32)
    block = jnp.einsum("mn,knc->kmc", forward, taps, preferred_element_type=F32)
    parity = jnp.where(jnp.arange(2 * length) % length < length // 2, 1.0, -1.0)[None, :, None]
    before = jnp.concatenate([jnp.zeros_like(data[:1]), data[:-1]], axis=0)
    pair = before + parity * data
    edge = (jnp.arange(length) == 0)[None, :, None]
    real = jnp.zeros_like(data[:, :length])
    imag = jnp.zeros_like(real)
    for lag in range(min(win, spans)):
        own = jnp.concatenate([jnp.zeros_like(pair[:lag]), pair[: spans - lag]], axis=0)
        own_real, own_imag = own[:, :length], own[:, length:]
        tap_real, tap_imag = block[lag, :length][None], block[lag, length:][None]
        first, second = tap_real * own_real, tap_imag * own_imag
        real = real + jnp.where(edge, first, first - second)
        imag = imag + jnp.where(edge, second, tap_real * own_imag + tap_imag * own_real)
    total = jnp.concatenate([real, imag], axis=1).astype(BF16)
    return jnp.einsum("im,kmc->kic", inverse, total, preferred_element_type=F32)


def plain_body(forward, inverse, query_gate, key_gate, value_in, filter_taps, skip_gain, out_weight):
    length, width = query_gate.shape
    devices = lax.axis_size("ctx")
    share = width // devices
    mixed_in = (key_gate.astype(F32) * value_in.astype(F32)).astype(BF16)
    x = lax.all_to_all(mixed_in, "ctx", split_axis=1, concat_axis=0, tiled=True)
    taps = lax.dynamic_slice_in_dim(filter_taps, lax.axis_index("ctx") * share, share, axis=1)
    conv = long_conv(
        x.reshape(devices, length, share),
        taps.astype(BF16).reshape(-1, length, share),
        forward,
        inverse,
    )
    conv = conv.astype(BF16).reshape(devices * length, share)
    conv = lax.all_to_all(conv, "ctx", split_axis=0, concat_axis=1, tiled=True)
    combined = conv.astype(F32) + skip_gain[None, :] * mixed_in.astype(F32)
    gated = (query_gate.astype(F32) * combined).astype(BF16)
    partial_value = jnp.dot(gated, out_weight, preferred_element_type=F32)
    return lax.psum_scatter(partial_value.astype(BF16), "ch", scatter_dimension=1, tiled=True)


def solution(mesh):
    in_specs = (
        P("ctx", "ch"),
        P("ctx", "ch"),
        P("ctx", "ch"),
        P(None, "ch"),
        P("ch"),
        P("ch", None),
    )
    out_specs = P("ctx", "ch")

    def whole(query_gate, *rest):
        length = query_gate.shape[0] // mesh.shape["ctx"]
        forward, inverse = transform_tables(length)

        def body(*args):
            return plain_body(forward, inverse, *args)

        return jax.shard_map(
            body, mesh=mesh, in_specs=in_specs, out_specs=out_specs, check_vma=False
        )(query_gate, *rest)

    return whole
```

profile of v0, /device:TPU:0, one launch (start us, length us, event | category | flops | bytes accessed | tf_op | source)
XLA Modules:
  0.0 155.8 jit_solution(2799826418058103367)
XLA Ops:
  6.5 1.9 %multiply_convert_fusion.1 = bf16[512,1024]{1,0:T(8,128)(2,1)S(1)} fusion(bf16[512,1024]{1,0:T(8,128)(2,1)} %param.11, bf16[512,1024]{1,0:T(8,128)(2,1)} %param.10), kind=kLoop, calls=%fused_computation.40 | loop fusion | flops 2097152 | bytes 3145728 | tf_op jit(solution)/shard_map/convert_element_type | solution.py:54
  8.5 1.3 copy.13
  9.8 7.4 %all-to-all-start = ((bf16[512,8,128]{0,2,1:T(8,128)(2,1)}), bf16[512,8,128]{0,2,1:T(8,128)(2,1)S(1)}, u32[]{:S(2)}, u32[]{:S(2)}) async-start(bf16[512,8,128]{0,2,1:T(8,128)(2,1)} %bitcast.4), calls=%async_computation | async-start | bytes 2097152 | tf_op jit(solution)/shard_map/all_to_all | solution.py:55
  17.3 1.7 %dynamic-slice_convert_fusion = bf16[4096,128]{1,0:T(8,128)(2,1)S(1)} fusion(f32[4096,1024]{1,0:T(8,128)} %param.12, s32[]{:T(128)S(6)} %select_n.71), kind=kLoop, calls=%fused_computation.41 | loop fusion | bytes 2097156 | tf_op jit(solution)/shard_map/convert_element_type | solution.py:59
  19.0 1.3 convolution_bitcast_fusion.1
  20.3 2.0 %slice_bitcast_fusion.15 = (f32[512,128]{0,1:T(8,128)}, f32[512,128]{0,1:T(8,128)}, f32[512,128]{0,1:T(8,128)}, f32[512,128]{0,1:T(8,128)}, f32[512,128]{0,1:T(8...) fusion(f32[8,1024,128]{1,2,0:T(8,128)S(1)} %convolution_bitcast, ...), kind=kLoop, calls=%fused_computation.62 | loop fusion | bytes 8388608 | tf_op jit(solution)/shard_map/mul | solution.py:43
  22.3 20.6 %all-to-all-done = bf16[512,8,128]{0,2,1:T(8,128)(2,1)S(1)} async-done(((bf16[512,8,128]{0,2,1:T(8,128)(2,1)}), bf16[512,8,128]{0,2,1:T(8,128)(2,1)S(1)}, u32[]{:S(2)}, u32[]{:S(2)}) %all-to-all-start) | async-done | bytes 1048608 | tf_op jit(solution)/shard_map/all_to_all | solution.py:55
  43.0 1.3 convolution_bitcast_fusion
  44.3 0.5 slice.161
  44.7 1.0 multiply_add_fusion
  45.8 1.0 slice.181
  46.8 0.2 slice.178
  47.0 0.2 slice.175
  47.2 0.3 slice.172
  47.6 0.4 slice.169
  48.0 0.5 slice.166
  48.5 5.7 %add_convert_fusion = bf16[8,512,128]{1,2,0:T(8,128)(2,1)} fusion(f32[8,1024,128]{1,2,0:T(8,128)S(1)} %multiply_add_fusion, f32[7,1024,128]{1,2,0:T(8,128)S(1)} %slice.166, f32[6,1024,128]{1,2,0:T(8,128)S(1)} %slice.169, f32[5,1024,128]{1,2,0:T(8,128)S(1)} %slice.172, f32[4,1024,128]{1,2,0:T(8,128)S(1)} %slice.175, f32[3,1024,128]{1,2,0:T(8,128)S(1)} %slice.178, ...), kind=kLoop, calls=%fused_computation.39 | loop fusion | flops 25165824 | bytes 24117760 | tf_op jit(solution)/shard_map/convert.3 | solution.py:89
  54.1 5.7 %fusion.7 = bf16[8,512,128]{1,2,0:T(8,128)(2,1)} fusion(f32[8,1024,128]{1,2,0:T(8,128)S(1)} %multiply_add_fusion, f32[7,1024,128]{1,2,0:T(8,128)S(1)} %slice.166, f32[6,1024,128]{1,2,0:T(8,128)S(1)} %slice.169, f32[5,1024,128]{1,2,0:T(8,128)S(1)} %slice.172, f32[4,1024,128]{1,2,0:T(8,128)S(1)} %slice.175, f32[3,1024,128]{1,2,0:T(8,128)S(1)} %slice.178, ...), kind=kLoop, calls=%fused_computation.33 | loop fusion | flops 20971520 | bytes 24117760 | tf_op jit(solution)/shard_map/convert.2 | solution.py:89
  59.8 3.1 %fusion.15 = bf16[8,512,128]{1,2,0:T(8,128)(2,1)S(1)} fusion(bf16[512,1024,1]{1,0,2:T(8,128)(2,1)} %constant.65, bf16[8,512,128]{1,2,0:T(8,128)(2,1)} %add_convert_fusion, bf16[8,512,128]{1,2,0:T(8,128)(2,1)} %fusion.7), kind=kOutput, calls=%fused_computation.44 | convolution fusion | flops 1078460416 | bytes 4194304 | tf_op jit(solution)/shard_map/im,kmc->kic/dot_general | solution.py:47
  63.0 29.3 %all_to_all.26 = bf16[8,512,128]{1,2,0:T(8,128)(2,1)S(1)} all-to-all(bf16[8,512,128]{1,2,0:T(8,128)(2,1)S(1)} %fusion.15), channel_id=1, replica_groups=mesh['ctx'=8,'ch'=4] {'ctx'}, dimensions={0} | all-to-all | bytes 2097152 | tf_op jit(solution)/shard_map/all_to_all | solution.py:64
  92.2 0.3 convert_element_type.54
  92.6 1.9 %copy.14 = f32[512,1024]{1,0:T(8,128)} copy(f32[512,1024]{0,1:T(8,128)S(1)} %bitcast.53) | data formatting | bytes 4194304 | tf_op jit(solution)/shard_map/convert_element_type | solution.py:65
  94.4 10.8 %convolution_convert_fusion = bf16[512,4096]{1,0:T(8,128)(2,1)} fusion(bf16[1024,4096]{1,0:T(8,128)(2,1)} %param.14, f32[512,1024]{1,0:T(8,128)} %copy.14, bf16[512,1024]{1,0:T(8,128)(2,1)S(1)} %copy-done.1, bf16[512,1024]{1,0:T(8,128)(2,1)} %param.9, f32[1024]{0:T(1024)S(1)} %copy-done.3), kind=kOutput, calls=%fused_computation | convolution fusion | flops 4300210176 | bytes 16781312 | tf_op jit(solution)/shard_map/dot_general | solution.py:67
  105.2 43.7 %reduce-scatter.2.cloned.1.call-done = bf16[512,1024]{1,0:T(8,128)(2,1)} async-done(((bf16[512,4096]{1,0:T(8,128)(2,1)}), bf16[512,1024]{1,0:T(8,128)(2,1)}) %reduce-scatter.2.cloned.1.call-update) | async-done | bytes 1048592 | tf_op jit(solution)/shard_map/reduce_scatter | solution.py:68
  (13 shorter events, 0.1 us)
Async XLA Ops:
  8.5 1.3 copy-start
  9.8 9.2 %copy-start.2 = (bf16[1024,512,1]{1,0,2:T(8,128)(2,1)S(1)}, bf16[1024,512,1]{1,0,2:T(8,128)(2,1)}, u32[]{:S(2)}) copy-start(bf16[1024,512,1]{1,0,2:T(8,128)(2,1)} %constant.64) | copy-start | bytes 3145732
  9.8 33.2 %all-to-all-start = ((bf16[512,8,128]{0,2,1:T(8,128)(2,1)}), bf16[512,8,128]{0,2,1:T(8,128)(2,1)S(1)}, u32[]{:S(2)}, u32[]{:S(2)}) async-start(bf16[512,8,128]{0,2,1:T(8,128)(2,1)} %bitcast.4), calls=%async_computation | async-start | bytes 2097152 | tf_op jit(solution)/shard_map/all_to_all | solution.py:55
  17.2 131.8 %reduce-scatter.2.cloned.1.call-start = ((), (), s32[]{:S(2)}) async-start(), calls=%async_computation.3 | async-start | bytes 5242880 | tf_op jit(solution)/shard_map/reduce_scatter | solution.py:68
  92.5 1.9 %copy-start.1 = (bf16[512,1024]{1,0:T(8,128)(2,1)S(1)}, bf16[512,1024]{1,0:T(8,128)(2,1)}, u32[]{:S(2)}) copy-start(bf16[512,1024]{1,0:T(8,128)(2,1)} %copy-done) | copy-start | bytes 3145732
  92.5 1.9 %copy-start.3 = (f32[1024]{0:T(1024)S(1)}, f32[1024]{0:T(1024)}, u32[]{:S(2)}) copy-start(f32[1024]{0:T(1024)} %param.13) | copy-start | bytes 12292
Sparse Core Ops, SparseCore 0:
  105.4 43.5 reduce-scatter.1
where the time goes:
time: 156 us
  waiting for transfers between devices  64.4 us (41%)
  blocking collectives  29.3 us (19%)
  matrix products  16.5 us (11%)
  other arithmetic  14.5 us (9%)
  between operations  13.6 us (9%)
  local copies, waits for them, and re-layouts  10.1 us (6%)
  starting transfers between devices  7.42 us (5%)
    reduce_scatter x1, waiting for transfers between devices, plain_body(): lax.psum_scatter(partial_value.astype(BF16), 'ch', scatter_dimension=1, t...  43.7 us
    all_to_all x1, blocking collectives, plain_body(): conv = lax.all_to_all(conv, 'ctx', split_axis=0, concat_axis=1, tiled=True)  29.3 us
    all_to_all x1, waiting for transfers between devices, plain_body(): x = lax.all_to_all(mixed_in, 'ctx', split_axis=1, concat_axis=0, tiled=True)  20.6 us
    another operation x2, other arithmetic, whole(): jax.shard_map(body, mesh=mesh, in_specs=in_specs, out_specs=out_specs, ch...  11.3 us
    dot_general x1, matrix products, plain_body(): partial_value = jnp.dot(gated, out_weight, preferred_element_type=F32)  10.8 us
    all_to_all x1, starting transfers between devices, plain_body(): x = lax.all_to_all(mixed_in, 'ctx', split_axis=1, concat_axis=0, tiled=True)  7.38 us
    dot_general x1, matrix products, long_conv(): return jnp.einsum('im,kmc->kic', inverse, total, preferred_element_type=F32)  3.14 us
  transfers between devices with their start and end apart: 2, of which 2 were waited for; matrix products, arithmetic and copies ran while one was open for 3% of the time, Pallas kernels for 0%

commit v1 on v0

--- a/solution.py
+++ b/solution.py
@@ -1,9 +1,13 @@
+import functools
+
 import ml_dtypes
 import numpy as np
 
 import jax
 import jax.numpy as jnp
 from jax import lax
+from jax.experimental import pallas as pl
+from jax.experimental.pallas import tpu as pltpu
 from jax.sharding import PartitionSpec as P
 
 BF16 = jnp.bfloat16
@@ -68,6 +72,299 @@
     return lax.psum_scatter(partial_value.astype(BF16), "ch", scatter_dimension=1, tiled=True)
 
 
+MESH = pl.DeviceIdType.MESH
+CHUNKS = 4
+ROWS = 8
+
+
+def spectral_tile(row, sign, edge, taps_ref, data_ref, total_ref):
+    pairs, height, lanes = data_ref.shape
+    share, spans = lanes // 2, 2 * pairs
+    real_rows, imag_rows = pl.ds(row, ROWS), pl.ds(row + height // 2, ROWS)
+
+    def parts(ref, index):
+        cols = slice((index % 2) * share, (index % 2 + 1) * share)
+        return ref[index // 2, real_rows, cols], ref[index // 2, imag_rows, cols]
+
+    taps = [parts(taps_ref, j) for j in range(2 * taps_ref.shape[0])]
+    own, before = [], None
+    for span in range(spans):
+        here = parts(data_ref, span)
+        if before is None:
+            own.append(here if sign > 0 else tuple(-part for part in here))
+        elif sign > 0:
+            own.append(tuple(b + h for b, h in zip(before, here)))
+        else:
+            own.append(tuple(b - h for b, h in zip(before, here)))
+        before = here
+    for span in range(spans):
+        first = second = cross = None
+        for lag in range(min(span + 1, len(taps))):
+            (tr, ti), (xr, xi) = taps[lag], own[span - lag]
+            if lag == 0:
+                first, second, cross = tr * xr, ti * xi, tr * xi + ti * xr
+            else:
+                first, second = first + tr * xr, second + ti * xi
+                cross = cross + tr * xi + ti * xr
+        real, imag = first - second, cross
+        if edge:
+            at_edge = lax.broadcasted_iota(jnp.int32, real.shape, 0) == 0
+            real, imag = jnp.where(at_edge, first, real), jnp.where(at_edge, second, imag)
+        cols = slice((span % 2) * share, (span % 2 + 1) * share)
+        total_ref[span // 2, real_rows, cols] = real
+        total_ref[span // 2, imag_rows, cols] = imag
+
+
+def fused_kernel(
+    n, q_hbm, k_hbm, v_hbm, taps_hbm, skip_ref, w_hbm, fwd_hbm, inv_hbm, out_ref,
+    q_ref, k_ref, v_ref, taps_ref, w_ref, fwd_ref, inv_ref,
+    mixed, recv1, spec_b, spec_x, total, total_b, send2, recv2, gated, s1, r1, s2, r2, acc,
+    load_sem, own1_sem, own2_sem, a_send, a_recv, b_send, b_recv, c_send, c_recv, d_send, d_recv,
+):
+    me, ch = lax.axis_index("ctx"), lax.axis_index("ch")
+    y, core = ch // 2, ch % 2
+    beside, across = y * 2 + 1 - core, (1 - y) * 2 + core
+    opposite = (1 - y) * 2 + 1 - core
+    length, width = q_hbm.shape
+    share, depth = width // n, length // CHUNKS
+    offsets = sorted(range(1, n), key=lambda o: abs(o - n // 2))
+
+    def load(index, src, dst):
+        copy = pltpu.make_async_copy(src, dst, load_sem.at[index])
+        copy.start()
+        return copy
+
+    taps_cols = pl.ds(pl.multiple_of(me * share, share), share)
+    load_k, load_v = load(0, k_hbm, k_ref), load(1, v_hbm, v_ref)
+    load_fwd = load(2, fwd_hbm, fwd_ref)
+    load_taps = load(3, taps_hbm.at[:, taps_cols], taps_ref)
+    load_inv, load_q = load(4, inv_hbm, inv_ref), load(5, q_hbm, q_ref)
+    load_w = [
+        load(6 + i, w_hbm.at[:, pl.ds(pl.multiple_of(owner * width, width), width)], w_ref.at[i])
+        for i, owner in enumerate((opposite, beside, across, ch))
+    ]
+
+    barrier = pltpu.get_barrier_semaphore()
+    for o in offsets:
+        peer = {"ctx": lax.rem(me + o, n)}
+        pl.semaphore_signal(barrier, inc=1, device_id=peer, device_id_type=MESH)
+    for other in (beside, across):
+        pl.semaphore_signal(barrier, inc=1, device_id={"ch": other}, device_id_type=MESH)
+
+    load_k.wait()
+    load_v.wait()
+    for d in range(n):
+        cols = slice(d * share, (d + 1) * share)
+        mixed[d] = (k_ref[:, cols].astype(F32) * v_ref[:, cols].astype(F32)).astype(BF16)
+    pl.semaphore_wait(barrier, n + 1)
+
+    def half(index):
+        return pl.ds(pl.multiple_of(lax.rem(index, 2) * share, share), share)
+
+    def span_copy(peer, src, landing, sem_out, sem_in):
+        return pltpu.make_async_remote_copy(
+            src_ref=mixed.at[src],
+            dst_ref=recv1.at[landing // 2, :, half(landing)],
+            send_sem=a_send.at[sem_out],
+            recv_sem=a_recv.at[sem_in],
+            device_id={"ctx": peer},
+            device_id_type=MESH,
+        )
+
+    sends = []
+    for o in offsets:
+        peer = lax.rem(me + o, n)
+        copy = span_copy(peer, peer, me, o - 1, me)
+        copy.start()
+        sends.append(copy)
+    own = pltpu.make_async_copy(mixed.at[me], recv1.at[me // 2, :, half(me)], own1_sem)
+    own.start()
+
+    load_fwd.wait()
+    load_taps.wait()
+    for p in range(spec_b.shape[0]):
+        blocks = [taps_ref[(2 * p + i) * length : (2 * p + i + 1) * length] for i in range(2)]
+        spec_b[p] = jnp.dot(
+            fwd_ref[...], jnp.concatenate(blocks, axis=1).astype(BF16), preferred_element_type=F32
+        )
+    own.wait()
+    for p in range(n // 2):
+        for src in (2 * p, 2 * p + 1):
+
+            @pl.when(src != me)
+            def _():
+                cols = slice((src % 2) * share, (src % 2 + 1) * share)
+                pltpu.make_async_remote_copy(
+                    src_ref=mixed.at[src],
+                    dst_ref=recv1.at[src // 2, :, cols],
+                    send_sem=a_send.at[0],
+                    recv_sem=a_recv.at[src],
+                    device_id={"ctx": lax.rem(me + 1, n)},
+                    device_id_type=MESH,
+                ).wait_recv()
+
+        spec_x[p] = jnp.dot(fwd_ref[...], recv1[p], preferred_element_type=F32)
+
+    spectral_tile(0, 1, True, spec_b, spec_x, total)
+    tiles = length // 2 // ROWS
+
+    def even(i, carry):
+        spectral_tile(pl.multiple_of(i * ROWS, ROWS), 1, False, spec_b, spec_x, total)
+        return carry
+
+    def odd(i, carry):
+        spectral_tile(pl.multiple_of(i * ROWS, ROWS), -1, False, spec_b, spec_x, total)
+        return carry
+
+    lax.fori_loop(1, tiles, even, 0)
+    lax.fori_loop(tiles, 2 * tiles, odd, 0)
+    for p in range(n // 2):
+        total_b[p] = total[p].astype(BF16)
+
+    load_inv.wait()
+    own_copies = []
+    for t in range(CHUNKS):
+        rows = slice(t * depth, (t + 1) * depth)
+        for p in range(n // 2):
+            conv = jnp.dot(inv_ref[rows], total_b[p], preferred_element_type=F32).astype(BF16)
+            send2[t, 2 * p] = conv[:, :share]
+            send2[t, 2 * p + 1] = conv[:, share:]
+        for o in offsets:
+            peer = lax.rem(me + o, n)
+            copy = pltpu.make_async_remote_copy(
+                src_ref=send2.at[t, peer],
+                dst_ref=recv2.at[rows, taps_cols],
+                send_sem=b_send.at[t, o - 1],
+                recv_sem=b_recv.at[t, o - 1],
+                device_id={"ctx": peer},
+                device_id_type=MESH,
+            )
+            copy.start()
+            sends.append(copy)
+        copy = pltpu.make_async_copy(send2.at[t, me], recv2.at[rows, taps_cols], own2_sem.at[t])
+        copy.start()
+        own_copies.append(copy)
+
+    def exchange(src, dst, out_sem, in_sem, other):
+        copy = pltpu.make_async_remote_copy(
+            src_ref=src,
+            dst_ref=dst,
+            send_sem=out_sem,
+            recv_sem=in_sem,
+            device_id={"ch": other},
+            device_id_type=MESH,
+        )
+        copy.start()
+        sends.append(copy)
+        return copy
+
+    def project(block):
+        return jnp.dot(gated[...], w_ref[block], preferred_element_type=F32)
+
+    def finish(t, copy):
+        copy.wait_recv()
+        rows = slice(t * depth, (t + 1) * depth)
+        out_ref[rows] = (acc[t] + r2[t].astype(F32)).astype(BF16)
+
+    load_q.wait()
+    for copy in load_w:
+        copy.wait()
+    last = None
+    for t in range(CHUNKS):
+        rows = slice(t * depth, (t + 1) * depth)
+        own_copies[t].wait()
+        for o in offsets:
+            src = lax.rem(me + n - o, n)
+            pltpu.make_async_remote_copy(
+                src_ref=send2.at[t, src],
+                dst_ref=recv2.at[rows, pl.ds(pl.multiple_of(src * share, share), share)],
+                send_sem=b_send.at[t, o - 1],
+                recv_sem=b_recv.at[t, o - 1],
+                device_id={"ctx": src},
+                device_id_type=MESH,
+            ).wait_recv()
+        for d in range(n):
+            cols = slice(d * share, (d + 1) * share)
+            conv = recv2[rows, cols].astype(F32)
+            conv = conv + skip_ref[:, cols] * mixed[d, rows].astype(F32)
+            gated[:, cols] = (q_ref[rows, cols].astype(F32) * conv).astype(BF16)
+        s1[t, 0] = project(0).astype(BF16)
+        far = exchange(s1.at[t, 0], r1.at[t, 0], c_send.at[t, 0], c_recv.at[t, 0], beside)
+        s1[t, 1] = project(1).astype(BF16)
+        near = exchange(s1.at[t, 1], r1.at[t, 1], c_send.at[t, 1], c_recv.at[t, 1], beside)
+        passed = project(2)
+        far.wait_recv()
+        s2[t] = (passed + r1[t, 0].astype(F32)).astype(BF16)
+        final = exchange(s2.at[t], r2.at[t], d_send.at[t], d_recv.at[t], across)
+        kept = project(3)
+        near.wait_recv()
+        acc[t] = kept + r1[t, 1].astype(F32)
+        if last is not None:
+            finish(t - 1, last)
+        last = final
+    finish(CHUNKS - 1, last)
+    for copy in sends:
+        copy.wait_send()
+
+
+def fused_body(forward, inverse, query_gate, key_gate, value_in, filter_taps, skip_gain, out_weight):
+    length, width = query_gate.shape
+    n = lax.axis_size("ctx")
+    share, depth, taps = width // n, length // CHUNKS, filter_taps.shape[0]
+    dma = pltpu.SemaphoreType.DMA
+    anywhere = pl.BlockSpec(memory_space=pl.ANY)
+    vmem = pl.BlockSpec(memory_space=pltpu.VMEM)
+    return pl.pallas_call(
+        functools.partial(fused_kernel, n),
+        out_shape=jax.ShapeDtypeStruct((length, width), BF16),
+        in_specs=[anywhere] * 4 + [vmem] + [anywhere] * 3,
+        out_specs=vmem,
+        scratch_shapes=[
+            pltpu.VMEM((length, width), BF16),
+            pltpu.VMEM((length, width), BF16),
+            pltpu.VMEM((length, width), BF16),
+            pltpu.VMEM((taps, share), F32),
+            pltpu.VMEM((4, width, width), BF16),
+            pltpu.VMEM((2 * length, length), BF16),
+            pltpu.VMEM((length, 2 * length), BF16),
+            pltpu.VMEM((n, length, share), BF16),
+            pltpu.VMEM((n // 2, length, 2 * share), BF16),
+            pltpu.VMEM((taps // length // 2, 2 * length, 2 * share), F32),
+            pltpu.VMEM((n // 2, 2 * length, 2 * share), F32),
+            pltpu.VMEM((n // 2, 2 * length, 2 * share), F32),
+            pltpu.VMEM((n // 2, 2 * length, 2 * share), BF16),
+            pltpu.VMEM((CHUNKS, n, depth, share), BF16),
+            pltpu.VMEM((length, width), BF16),
+            pltpu.VMEM((depth, width), BF16),
+            pltpu.VMEM((CHUNKS, 2, depth, width), BF16),
+            pltpu.VMEM((CHUNKS, 2, depth, width), BF16),
+            pltpu.VMEM((CHUNKS, depth, width), BF16),
+            pltpu.VMEM((CHUNKS, depth, width), BF16),
+            pltpu.VMEM((CHUNKS, depth, width), F32),
+            dma((10,)),
+            dma,
+            dma((CHUNKS,)),
+            dma((n - 1,)),
+            dma((n,)),
+            dma((CHUNKS, n - 1)),
+            dma((CHUNKS, n - 1)),
+            dma((CHUNKS, 2)),
+            dma((CHUNKS, 2)),
+            dma((CHUNKS,)),
+            dma((CHUNKS,)),
+        ],
+        compiler_params=pltpu.CompilerParams(
+            collective_id=0, has_side_effects=True, vmem_limit_bytes=56 * 2**20
+        ),
+        cost_estimate=pl.CostEstimate(
+            flops=10 * 10**9, bytes_accessed=16 * 2**20, transcendentals=0
+        ),
+    )(
+        query_gate, key_gate, value_in, filter_taps, skip_gain.reshape(1, width), out_weight,
+        forward, inverse,
+    )
+
+
 def solution(mesh):
     in_specs = (
         P("ctx", "ch"),
@@ -81,10 +378,15 @@
 
     def whole(query_gate, *rest):
         length = query_gate.shape[0] // mesh.shape["ctx"]
+        width = query_gate.shape[1] // mesh.shape["ch"]
         forward, inverse = transform_tables(length)
+        taps = rest[2].shape[0] // length
+        fits = mesh.shape["ch"] == 4 and width == 128 * mesh.shape["ctx"]
+        fits = fits and mesh.shape["ctx"] % 2 == 0 and taps % 2 == 0 and length % 128 == 0
+        chosen = fused_body if fits else plain_body
 
         def body(*args):
-            return plain_body(forward, inverse, *args)
+            return chosen(jnp.asarray(forward), jnp.asarray(inverse), *args)
 
         return jax.shard_map(
             body, mesh=mesh, in_specs=in_specs, out_specs=out_specs, check_vma=False

time: 156 us -> 76.1 us (0.49)
  Pallas kernels: 0 us -> 72.8 us
  waiting for transfers between devices: 64.4 us -> 0 us
  blocking collectives: 29.3 us -> 0 us
  matrix products: 16.5 us -> 0 us
  other arithmetic: 14.5 us -> 0 us
  between operations: 13.6 us -> 0.01 us
  local copies, waits for them, and re-layouts: 10.1 us -> 2.26 us
  starting transfers between devices: 7.42 us -> 0 us
    pallas_call x0 -> x1, Pallas kernels: none -> 72.8 us  [fused_body(): pl.pallas_call(functools.partial(fused_kernel, n), out_shape=jax.ShapeDty...]
    reduce_scatter x1 -> x0, waiting for transfers between devices: 43.7 us -> none  [plain_body(): lax.psum_scatter(partial_value.astype(BF16), 'ch', scatter_dimension=1, t...]
    all_to_all x1 -> x0, blocking collectives: 29.3 us -> none  [plain_body(): conv = lax.all_to_all(conv, 'ctx', split_axis=0, concat_axis=1, tiled=True)]
    all_to_all x1 -> x0, waiting for transfers between devices: 20.6 us -> none  [plain_body(): x = lax.all_to_all(mixed_in, 'ctx', split_axis=1, concat_axis=0, tiled=True)]
    dot_general x4 -> x0, matrix products: 16.5 us -> none  [the longest x1 10.8 us: plain_body(): partial_value = jnp.dot(gated, out_weight, preferred_element_type=F32)]
    another operation x2 -> x0, other arithmetic: 11.3 us -> none  [whole(): jax.shard_map(body, mesh=mesh, in_specs=in_specs, out_specs=out_specs, ch...]
    all_to_all x1 -> x0, starting transfers between devices: 7.38 us -> none  [plain_body(): x = lax.all_to_all(mixed_in, 'ctx', split_axis=1, concat_axis=0, tiled=True)]
    convert_element_type x3 -> x0, local copies, waits for them, and re-layouts: 4.88 us -> none  [the longest x1 1.86 us: plain_body(): combined = conv.astype(F32) + skip_gain[None, :] * mixed_in.astype(F32)]
  transfers between devices with their start and end apart: 2 -> 0, of which waited for: 2 -> 0; matrix products, arithmetic and copies ran while one was open for 3% -> 0% of each run, Pallas kernels for 0% -> 0%
where the time goes in v1:
time: 76.1 us; the launch traced here: 75.1 us
  Pallas kernels  72.8 us (96%)
  local copies, waits for them, and re-layouts  2.26 us (3%)
    pallas_call x1, Pallas kernels, fused_body(): pl.pallas_call(functools.partial(fused_kernel, n), out_shape=jax.ShapeDty...  72.8 us
    unnamed x1, local copies, waits for them, and re-layouts  2.26 us

profile of v1, /device:TPU:0, one launch (start us, length us, event | category | flops | bytes accessed | tf_op | source)
XLA Modules:
  0.0 75.1 jit_solution(700441981220064840)
XLA Ops:
  0.0 72.8 %shard_map.82 = bf16[512,1024]{1,0:T(8,128)(2,1)} custom-call(bf16[512,1024]{1,0:T(8,128)(2,1)} %q_hbm.1, bf16[512,1024]{1,0:T(8,128)(2,1)} %k_hbm.1, bf16[512,1024]{1,0:T(8,128)(2,1)} %v_hbm.1, f32[4096,1024]{1,0:T(8,128)} %taps_hbm.1, f32[1,1024]{1,0:T(1,128)} %bitcast.1, bf16[1024,4096]{1,0:T(8,128)(2,1)} %w_hbm.1, ...), custom_call_target="tpu_custom_call" | custom-call | flops 10000000000 | bytes 16777216 | tf_op jit(solution)/shard_map/pallas_call | solution.py:317
  72.8 2.3 %copy.10 = bf16[512,1024]{1,0:T(8,128)(2,1)} copy(bf16[512,1024]{1,0:T(8,128)(2,1)} %shard_map.82) | data formatting | bytes 2097152

commit v2 on v1

--- a/solution.py
+++ b/solution.py
@@ -73,46 +73,80 @@
 
 
 MESH = pl.DeviceIdType.MESH
-CHUNKS = 4
+EIGHTHS = (2, 2, 2, 1, 1)
 ROWS = 8
 
 
-def spectral_tile(row, sign, edge, taps_ref, data_ref, total_ref):
+def spectral_tile(row, sign, edge, outs, ins, add, taps_ref, data_ref, total_ref):
     pairs, height, lanes = data_ref.shape
-    share, spans = lanes // 2, 2 * pairs
+    share, lags = lanes // 2, 2 * taps_ref.shape[0]
     real_rows, imag_rows = pl.ds(row, ROWS), pl.ds(row + height // 2, ROWS)
 
     def parts(ref, index):
         cols = slice((index % 2) * share, (index % 2 + 1) * share)
         return ref[index // 2, real_rows, cols], ref[index // 2, imag_rows, cols]
 
-    taps = [parts(taps_ref, j) for j in range(2 * taps_ref.shape[0])]
-    own, before = [], None
-    for span in range(spans):
+    used = sorted({o - i for o in outs for i in ins if 0 <= o - i < lags})
+    taps = {lag: parts(taps_ref, lag) for lag in used}
+    own = {}
+    before = parts(data_ref, ins[0] - 1) if ins[0] > 0 else None
+    for span in ins:
         here = parts(data_ref, span)
         if before is None:
-            own.append(here if sign > 0 else tuple(-part for part in here))
+            own[span] = here if sign > 0 else tuple(-part for part in here)
         elif sign > 0:
-            own.append(tuple(b + h for b, h in zip(before, here)))
+            own[span] = tuple(b + h for b, h in zip(before, here))
         else:
-            own.append(tuple(b - h for b, h in zip(before, here)))
+            own[span] = tuple(b - h for b, h in zip(before, here))
         before = here
-    for span in range(spans):
+    for out in outs:
         first = second = cross = None
-        for lag in range(min(span + 1, len(taps))):
-            (tr, ti), (xr, xi) = taps[lag], own[span - lag]
-            if lag == 0:
+        for span in ins:
+            if not 0 <= out - span < lags:
+                continue
+            (tr, ti), (xr, xi) = taps[out - span], own[span]
+            if first is None:
                 first, second, cross = tr * xr, ti * xi, tr * xi + ti * xr
             else:
                 first, second = first + tr * xr, second + ti * xi
                 cross = cross + tr * xi + ti * xr
+        cols = slice((out % 2) * share, (out % 2 + 1) * share)
+        if first is None:
+            if not add:
+                total_ref[out // 2, real_rows, cols] = jnp.zeros((ROWS, share), F32)
+                total_ref[out // 2, imag_rows, cols] = jnp.zeros((ROWS, share), F32)
+            continue
         real, imag = first - second, cross
         if edge:
             at_edge = lax.broadcasted_iota(jnp.int32, real.shape, 0) == 0
             real, imag = jnp.where(at_edge, first, real), jnp.where(at_edge, second, imag)
-        cols = slice((span % 2) * share, (span % 2 + 1) * share)
-        total_ref[span // 2, real_rows, cols] = real
-        total_ref[span // 2, imag_rows, cols] = imag
+        if add:
+            real += total_ref[out // 2, real_rows, cols]
+            imag += total_ref[out // 2, imag_rows, cols]
+        total_ref[out // 2, real_rows, cols] = real
+        total_ref[out // 2, imag_rows, cols] = imag
+
+
+def spectral_sums(outs, ins, add, taps_ref, data_ref, total_ref):
+    refs = (taps_ref, data_ref, total_ref)
+    tiles = data_ref.shape[1] // 4 // ROWS
+    spectral_tile(0, 1, True, outs, ins, add, *refs)
+
+    def even(i, carry):
+        spectral_tile(pl.multiple_of(i * ROWS, ROWS), 1, False, outs, ins, add, *refs)
+        return carry
+
+    def odd(i, carry):
+        spectral_tile(pl.multiple_of(i * ROWS, ROWS), -1, False, outs, ins, add, *refs)
+        return carry
+
+    lax.fori_loop(1, tiles, even, 0)
+    lax.fori_loop(tiles, 2 * tiles, odd, 0)
+
+
+def chunk_rows(length):
+    ends = np.cumsum((0,) + EIGHTHS) * (length // 8)
+    return [slice(int(a), int(b)) for a, b in zip(ends[:-1], ends[1:])]
 
 
 def fused_kernel(
@@ -126,8 +160,14 @@
     beside, across = y * 2 + 1 - core, (1 - y) * 2 + core
     opposite = (1 - y) * 2 + 1 - core
     length, width = q_hbm.shape
-    share, depth = width // n, length // CHUNKS
-    offsets = sorted(range(1, n), key=lambda o: abs(o - n // 2))
+    share, group = width // n, n // 2
+    chunks = chunk_rows(length)
+    side = me // group
+    here = [side * group + lax.rem(me + i, group) for i in range(group)]
+    there = [(1 - side) * group + lax.rem(me + i, group) for i in range(group)]
+    order = [there[0]]
+    for i in range(1, group):
+        order += [here[i], there[i]]
 
     def load(index, src, dst):
         copy = pltpu.make_async_copy(src, dst, load_sem.at[index])
@@ -145,9 +185,8 @@
     ]
 
     barrier = pltpu.get_barrier_semaphore()
-    for o in offsets:
-        peer = {"ctx": lax.rem(me + o, n)}
-        pl.semaphore_signal(barrier, inc=1, device_id=peer, device_id_type=MESH)
+    for peer in order:
+        pl.semaphore_signal(barrier, inc=1, device_id={"ctx": peer}, device_id_type=MESH)
     for other in (beside, across):
         pl.semaphore_signal(barrier, inc=1, device_id={"ch": other}, device_id_type=MESH)
 
@@ -161,20 +200,16 @@
     def half(index):
         return pl.ds(pl.multiple_of(lax.rem(index, 2) * share, share), share)
 
-    def span_copy(peer, src, landing, sem_out, sem_in):
-        return pltpu.make_async_remote_copy(
-            src_ref=mixed.at[src],
-            dst_ref=recv1.at[landing // 2, :, half(landing)],
-            send_sem=a_send.at[sem_out],
-            recv_sem=a_recv.at[sem_in],
+    sends = []
+    for i, peer in enumerate(order):
+        copy = pltpu.make_async_remote_copy(
+            src_ref=mixed.at[peer],
+            dst_ref=recv1.at[me // 2, :, half(me)],
+            send_sem=a_send.at[i],
+            recv_sem=a_recv.at[me],
             device_id={"ctx": peer},
             device_id_type=MESH,
         )
-
-    sends = []
-    for o in offsets:
-        peer = lax.rem(me + o, n)
-        copy = span_copy(peer, peer, me, o - 1, me)
         copy.start()
         sends.append(copy)
     own = pltpu.make_async_copy(mixed.at[me], recv1.at[me // 2, :, half(me)], own1_sem)
@@ -188,7 +223,8 @@
             fwd_ref[...], jnp.concatenate(blocks, axis=1).astype(BF16), preferred_element_type=F32
         )
     own.wait()
-    for p in range(n // 2):
+
+    def spectrum(p):
         for src in (2 * p, 2 * p + 1):
 
             @pl.when(src != me)
@@ -199,51 +235,59 @@
                     dst_ref=recv1.at[src // 2, :, cols],
                     send_sem=a_send.at[0],
                     recv_sem=a_recv.at[src],
-                    device_id={"ctx": lax.rem(me + 1, n)},
+                    device_id={"ctx": order[0]},
                     device_id_type=MESH,
                 ).wait_recv()
 
         spec_x[p] = jnp.dot(fwd_ref[...], recv1[p], preferred_element_type=F32)
 
-    spectral_tile(0, 1, True, spec_b, spec_x, total)
-    tiles = length // 2 // ROWS
-
-    def even(i, carry):
-        spectral_tile(pl.multiple_of(i * ROWS, ROWS), 1, False, spec_b, spec_x, total)
-        return carry
-
-    def odd(i, carry):
-        spectral_tile(pl.multiple_of(i * ROWS, ROWS), -1, False, spec_b, spec_x, total)
-        return carry
-
-    lax.fori_loop(1, tiles, even, 0)
-    lax.fori_loop(tiles, 2 * tiles, odd, 0)
-    for p in range(n // 2):
-        total_b[p] = total[p].astype(BF16)
-
+    def way_back(t, peer):
+        return pltpu.make_async_remote_copy(
+            src_ref=send2.at[peer, chunks[t]],
+            dst_ref=recv2.at[chunks[t], taps_cols],
+            send_sem=b_send.at[t, peer],
+            recv_sem=b_recv.at[t, me],
+            device_id={"ctx": peer},
+            device_id_type=MESH,
+        )
+
+    def own_rows(t):
+        return pltpu.make_async_copy(
+            send2.at[me, chunks[t]], recv2.at[chunks[t], taps_cols], own2_sem.at[t]
+        )
+
+    def send_back(which):
+        pairs = range(which * group // 2, (which + 1) * group // 2)
+        for p in pairs:
+            total_b[p] = total[p].astype(BF16)
+        for t, rows in enumerate(chunks):
+            for p in pairs:
+                conv = jnp.dot(inv_ref[rows], total_b[p], preferred_element_type=F32).astype(BF16)
+                send2[2 * p, rows] = conv[:, :share]
+                send2[2 * p + 1, rows] = conv[:, share:]
+
+            @pl.when(side == which)
+            def _():
+                own_rows(t).start()
+
+            @pl.when(side != which)
+            def _():
+                way_back(t, which * group + lax.rem(me, group)).start()
+
+            for i in range(1, group):
+                way_back(t, which * group + lax.rem(me + i, group)).start()
+
+    low, high = range(group), range(group, n)
+    for p in range(group // 2):
+        spectrum(p)
+    spectral_sums(low, low, False, spec_b, spec_x, total)
     load_inv.wait()
-    own_copies = []
-    for t in range(CHUNKS):
-        rows = slice(t * depth, (t + 1) * depth)
-        for p in range(n // 2):
-            conv = jnp.dot(inv_ref[rows], total_b[p], preferred_element_type=F32).astype(BF16)
-            send2[t, 2 * p] = conv[:, :share]
-            send2[t, 2 * p + 1] = conv[:, share:]
-        for o in offsets:
-            peer = lax.rem(me + o, n)
-            copy = pltpu.make_async_remote_copy(
-                src_ref=send2.at[t, peer],
-                dst_ref=recv2.at[rows, taps_cols],
-                send_sem=b_send.at[t, o - 1],
-                recv_sem=b_recv.at[t, o - 1],
-                device_id={"ctx": peer},
-                device_id_type=MESH,
-            )
-            copy.start()
-            sends.append(copy)
-        copy = pltpu.make_async_copy(send2.at[t, me], recv2.at[rows, taps_cols], own2_sem.at[t])
-        copy.start()
-        own_copies.append(copy)
+    send_back(0)
+    spectral_sums(high, low, False, spec_b, spec_x, total)
+    for p in range(group // 2, group):
+        spectrum(p)
+    spectral_sums(high, high, True, spec_b, spec_x, total)
+    send_back(1)
 
     def exchange(src, dst, out_sem, in_sem, other):
         copy = pltpu.make_async_remote_copy(
@@ -258,59 +302,66 @@
         sends.append(copy)
         return copy
 
-    def project(block):
-        return jnp.dot(gated[...], w_ref[block], preferred_element_type=F32)
+    def project(rows, block):
+        return jnp.dot(gated[rows], w_ref[block], preferred_element_type=F32)
 
     def finish(t, copy):
         copy.wait_recv()
-        rows = slice(t * depth, (t + 1) * depth)
-        out_ref[rows] = (acc[t] + r2[t].astype(F32)).astype(BF16)
+        out_ref[chunks[t]] = (acc[chunks[t]] + r2[chunks[t]].astype(F32)).astype(BF16)
 
     load_q.wait()
     for copy in load_w:
         copy.wait()
     last = None
-    for t in range(CHUNKS):
-        rows = slice(t * depth, (t + 1) * depth)
-        own_copies[t].wait()
-        for o in offsets:
-            src = lax.rem(me + n - o, n)
-            pltpu.make_async_remote_copy(
-                src_ref=send2.at[t, src],
-                dst_ref=recv2.at[rows, pl.ds(pl.multiple_of(src * share, share), share)],
-                send_sem=b_send.at[t, o - 1],
-                recv_sem=b_recv.at[t, o - 1],
-                device_id={"ctx": src},
-                device_id_type=MESH,
-            ).wait_recv()
+    for t, rows in enumerate(chunks):
+        own_rows(t).wait()
+        for src in range(n):
+
+            @pl.when(src != me)
+            def _():
+                cols = slice(src * share, (src + 1) * share)
+                pltpu.make_async_remote_copy(
+                    src_ref=send2.at[src, rows],
+                    dst_ref=recv2.at[rows, cols],
+                    send_sem=b_send.at[t, src],
+                    recv_sem=b_recv.at[t, src],
+                    device_id={"ctx": order[0]},
+                    device_id_type=MESH,
+                ).wait_recv()
+
         for d in range(n):
             cols = slice(d * share, (d + 1) * share)
             conv = recv2[rows, cols].astype(F32)
             conv = conv + skip_ref[:, cols] * mixed[d, rows].astype(F32)
-            gated[:, cols] = (q_ref[rows, cols].astype(F32) * conv).astype(BF16)
-        s1[t, 0] = project(0).astype(BF16)
-        far = exchange(s1.at[t, 0], r1.at[t, 0], c_send.at[t, 0], c_recv.at[t, 0], beside)
-        s1[t, 1] = project(1).astype(BF16)
-        near = exchange(s1.at[t, 1], r1.at[t, 1], c_send.at[t, 1], c_recv.at[t, 1], beside)
-        passed = project(2)
+            gated[rows, cols] = (q_ref[rows, cols].astype(F32) * conv).astype(BF16)
+        s1[0, rows] = project(rows, 0).astype(BF16)
+        far = exchange(s1.at[0, rows], r1.at[0, rows], c_send.at[t, 0], c_recv.at[t, 0], beside)
+        passed = project(rows, 2)
         far.wait_recv()
-        s2[t] = (passed + r1[t, 0].astype(F32)).astype(BF16)
-        final = exchange(s2.at[t], r2.at[t], d_send.at[t], d_recv.at[t], across)
-        kept = project(3)
+        s2[rows] = (passed + r1[0, rows].astype(F32)).astype(BF16)
+        final = exchange(s2.at[rows], r2.at[rows], d_send.at[t], d_recv.at[t], across)
+        s1[1, rows] = project(rows, 1).astype(BF16)
+        near = exchange(s1.at[1, rows], r1.at[1, rows], c_send.at[t, 1], c_recv.at[t, 1], beside)
+        kept = project(rows, 3)
         near.wait_recv()
-        acc[t] = kept + r1[t, 1].astype(F32)
+        acc[rows] = kept + r1[1, rows].astype(F32)
         if last is not None:
             finish(t - 1, last)
         last = final
-    finish(CHUNKS - 1, last)
+    finish(len(chunks) - 1, last)
     for copy in sends:
         copy.wait_send()
+    for t in range(len(chunks)):
+        for i in range(1, group):
+            way_back(t, here[i]).wait_send()
+        for peer in there:
+            way_back(t, peer).wait_send()
 
 
 def fused_body(forward, inverse, query_gate, key_gate, value_in, filter_taps, skip_gain, out_weight):
     length, width = query_gate.shape
     n = lax.axis_size("ctx")
-    share, depth, taps = width // n, length // CHUNKS, filter_taps.shape[0]
+    share, taps, chunks = width // n, filter_taps.shape[0], len(EIGHTHS)
     dma = pltpu.SemaphoreType.DMA
     anywhere = pl.BlockSpec(memory_space=pl.ANY)
     vmem = pl.BlockSpec(memory_space=pltpu.VMEM)
@@ -333,25 +384,25 @@
             pltpu.VMEM((n // 2, 2 * length, 2 * share), F32),
             pltpu.VMEM((n // 2, 2 * length, 2 * share), F32),
             pltpu.VMEM((n // 2, 2 * length, 2 * share), BF16),
-            pltpu.VMEM((CHUNKS, n, depth, share), BF16),
-            pltpu.VMEM((length, width), BF16),
-            pltpu.VMEM((depth, width), BF16),
-            pltpu.VMEM((CHUNKS, 2, depth, width), BF16),
-            pltpu.VMEM((CHUNKS, 2, depth, width), BF16),
-            pltpu.VMEM((CHUNKS, depth, width), BF16),
-            pltpu.VMEM((CHUNKS, depth, width), BF16),
-            pltpu.VMEM((CHUNKS, depth, width), F32),
+            pltpu.VMEM((n, length, share), BF16),
+            pltpu.VMEM((length, width), BF16),
+            pltpu.VMEM((length, width), BF16),
+            pltpu.VMEM((2, length, width), BF16),
+            pltpu.VMEM((2, length, width), BF16),
+            pltpu.VMEM((length, width), BF16),
+            pltpu.VMEM((length, width), BF16),
+            pltpu.VMEM((length, width), F32),
             dma((10,)),
             dma,
-            dma((CHUNKS,)),
+            dma((chunks,)),
             dma((n - 1,)),
             dma((n,)),
-            dma((CHUNKS, n - 1)),
-            dma((CHUNKS, n - 1)),
-            dma((CHUNKS, 2)),
-            dma((CHUNKS, 2)),
-            dma((CHUNKS,)),
-            dma((CHUNKS,)),
+            dma((chunks, n)),
+            dma((chunks, n)),
+            dma((chunks, 2)),
+            dma((chunks, 2)),
+            dma((chunks,)),
+            dma((chunks,)),
         ],
         compiler_params=pltpu.CompilerParams(
             collective_id=0, has_side_effects=True, vmem_limit_bytes=56 * 2**20
@@ -382,7 +433,7 @@
         forward, inverse = transform_tables(length)
         taps = rest[2].shape[0] // length
         fits = mesh.shape["ch"] == 4 and width == 128 * mesh.shape["ctx"]
-        fits = fits and mesh.shape["ctx"] % 2 == 0 and taps % 2 == 0 and length % 128 == 0
+        fits = fits and mesh.shape["ctx"] % 4 == 0 and taps % 2 == 0 and length % 128 == 0
         chosen = fused_body if fits else plain_body
 
         def body(*args):

time: 76.1 us -> 78.5 us (1.032)
  Pallas kernels: 72.8 us -> 76 us
    pallas_call x1, Pallas kernels: 72.8 us -> 76 us  [fused_body(): pl.pallas_call(functools.partial(fused_kernel, n), out_shape=jax.ShapeDty...]
where the time goes in v2:
time: 78.5 us; the launch traced here: 78.3 us
  Pallas kernels  76 us (97%)
  local copies, waits for them, and re-layouts  2.26 us (3%)
    pallas_call x1, Pallas kernels, fused_body(): pl.pallas_call(functools.partial(fused_kernel, n), out_shape=jax.ShapeDty...  76 us
    unnamed x1, local copies, waits for them, and re-layouts  2.26 us

profile of v2, /device:TPU:0, one launch (start us, length us, event | category | flops | bytes accessed | tf_op | source)
XLA Modules:
  0.0 78.3 jit_solution(18181261709373456821)
XLA Ops:
  0.0 76.0 %shard_map.82 = bf16[512,1024]{1,0:T(8,128)(2,1)} custom-call(bf16[512,1024]{1,0:T(8,128)(2,1)} %q_hbm.1, bf16[512,1024]{1,0:T(8,128)(2,1)} %k_hbm.1, bf16[512,1024]{1,0:T(8,128)(2,1)} %v_hbm.1, f32[4096,1024]{1,0:T(8,128)} %taps_hbm.1, f32[1,1024]{1,0:T(1,128)} %bitcast.1, bf16[1024,4096]{1,0:T(8,128)(2,1)} %w_hbm.1, ...), custom_call_target="tpu_custom_call" | custom-call | flops 10000000000 | bytes 16777216 | tf_op jit(solution)/shard_map/pallas_call | solution.py:368
  76.0 2.3 %copy.10 = bf16[512,1024]{1,0:T(8,128)(2,1)} copy(bf16[512,1024]{1,0:T(8,128)(2,1)} %shard_map.82) | data formatting | bytes 2097152

commit v3 on v2

--- a/solution.py
+++ b/solution.py
@@ -73,7 +73,7 @@
 
 
 MESH = pl.DeviceIdType.MESH
-EIGHTHS = (2, 2, 2, 1, 1)
+EIGHTHS = (2, 2, 2, 2)
 ROWS = 8
 
 
@@ -336,12 +336,12 @@
             gated[rows, cols] = (q_ref[rows, cols].astype(F32) * conv).astype(BF16)
         s1[0, rows] = project(rows, 0).astype(BF16)
         far = exchange(s1.at[0, rows], r1.at[0, rows], c_send.at[t, 0], c_recv.at[t, 0], beside)
+        s1[1, rows] = project(rows, 1).astype(BF16)
+        near = exchange(s1.at[1, rows], r1.at[1, rows], c_send.at[t, 1], c_recv.at[t, 1], beside)
         passed = project(rows, 2)
         far.wait_recv()
         s2[rows] = (passed + r1[0, rows].astype(F32)).astype(BF16)
         final = exchange(s2.at[rows], r2.at[rows], d_send.at[t], d_recv.at[t], across)
-        s1[1, rows] = project(rows, 1).astype(BF16)
-        near = exchange(s1.at[1, rows], r1.at[1, rows], c_send.at[t, 1], c_recv.at[t, 1], beside)
         kept = project(rows, 3)
         near.wait_recv()
         acc[rows] = kept + r1[1, rows].astype(F32)

time: 78.5 us -> 77.4 us (0.986)
  Pallas kernels: 76 us -> 74.9 us
    pallas_call x1, Pallas kernels: 76 us -> 74.9 us  [fused_body(): pl.pallas_call(functools.partial(fused_kernel, n), out_shape=jax.ShapeDty...]
where the time goes in v3:
time: 77.4 us; the launch traced here: 77.2 us
  Pallas kernels  74.9 us (97%)
  local copies, waits for them, and re-layouts  2.26 us (3%)
    pallas_call x1, Pallas kernels, fused_body(): pl.pallas_call(functools.partial(fused_kernel, n), out_shape=jax.ShapeDty...  74.9 us
    unnamed x1, local copies, waits for them, and re-layouts  2.26 us

profile of v3, /device:TPU:0, one launch (start us, length us, event | category | flops | bytes accessed | tf_op | source)
XLA Modules:
  0.0 77.2 jit_solution(11664878364525132536)
XLA Ops:
  0.0 74.9 %shard_map.82 = bf16[512,1024]{1,0:T(8,128)(2,1)} custom-call(bf16[512,1024]{1,0:T(8,128)(2,1)} %q_hbm.1, bf16[512,1024]{1,0:T(8,128)(2,1)} %k_hbm.1, bf16[512,1024]{1,0:T(8,128)(2,1)} %v_hbm.1, f32[4096,1024]{1,0:T(8,128)} %taps_hbm.1, f32[1,1024]{1,0:T(1,128)} %bitcast.1, bf16[1024,4096]{1,0:T(8,128)(2,1)} %w_hbm.1, ...), custom_call_target="tpu_custom_call" | custom-call | flops 10000000000 | bytes 16777216 | tf_op jit(solution)/shard_map/pallas_call | solution.py:368
  75.0 2.3 %copy.10 = bf16[512,1024]{1,0:T(8,128)(2,1)} copy(bf16[512,1024]{1,0:T(8,128)(2,1)} %shard_map.82) | data formatting | bytes 2097152

commit v4 on v3

--- a/solution.py
+++ b/solution.py
@@ -74,6 +74,7 @@
 
 MESH = pl.DeviceIdType.MESH
 EIGHTHS = (2, 2, 2, 2)
+AHEAD = 2
 ROWS = 8
 
 
@@ -256,6 +257,18 @@
             send2.at[me, chunks[t]], recv2.at[chunks[t], taps_cols], own2_sem.at[t]
         )
 
+    def launch(t, which):
+        @pl.when(side == which)
+        def _():
+            own_rows(t).start()
+
+        @pl.when(side != which)
+        def _():
+            way_back(t, which * group + lax.rem(me, group)).start()
+
+        for i in range(1, group):
+            way_back(t, which * group + lax.rem(me + i, group)).start()
+
     def send_back(which):
         pairs = range(which * group // 2, (which + 1) * group // 2)
         for p in pairs:
@@ -265,17 +278,8 @@
                 conv = jnp.dot(inv_ref[rows], total_b[p], preferred_element_type=F32).astype(BF16)
                 send2[2 * p, rows] = conv[:, :share]
                 send2[2 * p + 1, rows] = conv[:, share:]
-
-            @pl.when(side == which)
-            def _():
-                own_rows(t).start()
-
-            @pl.when(side != which)
-            def _():
-                way_back(t, which * group + lax.rem(me, group)).start()
-
-            for i in range(1, group):
-                way_back(t, which * group + lax.rem(me + i, group)).start()
+            if t < AHEAD:
+                launch(t, which)
 
     low, high = range(group), range(group, n)
     for p in range(group // 2):
@@ -338,6 +342,9 @@
         far = exchange(s1.at[0, rows], r1.at[0, rows], c_send.at[t, 0], c_recv.at[t, 0], beside)
         s1[1, rows] = project(rows, 1).astype(BF16)
         near = exchange(s1.at[1, rows], r1.at[1, rows], c_send.at[t, 1], c_recv.at[t, 1], beside)
+        if t + AHEAD < len(chunks):
+            launch(t + AHEAD, 0)
+            launch(t + AHEAD, 1)
         passed = project(rows, 2)
         far.wait_recv()
         s2[rows] = (passed + r1[0, rows].astype(F32)).astype(BF16)

time: 77.4 us -> 72.3 us (0.934)
  Pallas kernels: 74.9 us -> 69.5 us
    pallas_call x1, Pallas kernels: 74.9 us -> 69.5 us  [fused_body(): pl.pallas_call(functools.partial(fused_kernel, n), out_shape=jax.ShapeDty...]
where the time goes in v4:
time: 72.3 us; the launch traced here: 71.7 us
  Pallas kernels  69.5 us (96%)
  local copies, waits for them, and re-layouts  2.26 us (3%)
    pallas_call x1, Pallas kernels, fused_body(): pl.pallas_call(functools.partial(fused_kernel, n), out_shape=jax.ShapeDty...  69.5 us
    unnamed x1, local copies, waits for them, and re-layouts  2.26 us

profile of v4, /device:TPU:0, one launch (start us, length us, event | category | flops | bytes accessed | tf_op | source)
XLA Modules:
  0.0 71.7 jit_solution(9251762308972563561)
XLA Ops:
  0.0 69.5 %shard_map.82 = bf16[512,1024]{1,0:T(8,128)(2,1)} custom-call(bf16[512,1024]{1,0:T(8,128)(2,1)} %q_hbm.1, bf16[512,1024]{1,0:T(8,128)(2,1)} %k_hbm.1, bf16[512,1024]{1,0:T(8,128)(2,1)} %v_hbm.1, f32[4096,1024]{1,0:T(8,128)} %taps_hbm.1, f32[1,1024]{1,0:T(1,128)} %bitcast.1, bf16[1024,4096]{1,0:T(8,128)(2,1)} %w_hbm.1, ...), custom_call_target="tpu_custom_call" | custom-call | flops 10000000000 | bytes 16777216 | tf_op jit(solution)/shard_map/pallas_call | solution.py:375
  69.5 2.3 %copy.10 = bf16[512,1024]{1,0:T(8,128)(2,1)} copy(bf16[512,1024]{1,0:T(8,128)(2,1)} %shard_map.82) | data formatting | bytes 2097152

commit v5 on v4

--- a/solution.py
+++ b/solution.py
@@ -342,13 +342,13 @@
         far = exchange(s1.at[0, rows], r1.at[0, rows], c_send.at[t, 0], c_recv.at[t, 0], beside)
         s1[1, rows] = project(rows, 1).astype(BF16)
         near = exchange(s1.at[1, rows], r1.at[1, rows], c_send.at[t, 1], c_recv.at[t, 1], beside)
-        if t + AHEAD < len(chunks):
-            launch(t + AHEAD, 0)
-            launch(t + AHEAD, 1)
         passed = project(rows, 2)
         far.wait_recv()
         s2[rows] = (passed + r1[0, rows].astype(F32)).astype(BF16)
         final = exchange(s2.at[rows], r2.at[rows], d_send.at[t], d_recv.at[t], across)
+        if t + AHEAD < len(chunks):
+            launch(t + AHEAD, 0)
+            launch(t + AHEAD, 1)
         kept = project(rows, 3)
         near.wait_recv()
         acc[rows] = kept + r1[1, rows].astype(F32)

time: 72.3 us -> 76.1 us (1.053)
  Pallas kernels: 69.5 us -> 73.6 us
    pallas_call x1, Pallas kernels: 69.5 us -> 73.6 us  [fused_body(): pl.pallas_call(functools.partial(fused_kernel, n), out_shape=jax.ShapeDty...]
where the time goes in v5:
time: 76.1 us; the launch traced here: 75.9 us
  Pallas kernels  73.6 us (97%)
  local copies, waits for them, and re-layouts  2.26 us (3%)
    pallas_call x1, Pallas kernels, fused_body(): pl.pallas_call(functools.partial(fused_kernel, n), out_shape=jax.ShapeDty...  73.6 us
    unnamed x1, local copies, waits for them, and re-layouts  2.26 us

profile of v5, /device:TPU:0, one launch (start us, length us, event | category | flops | bytes accessed | tf_op | source)
XLA Modules:
  0.0 75.9 jit_solution(3325763034538898701)
XLA Ops:
  0.0 73.6 %shard_map.82 = bf16[512,1024]{1,0:T(8,128)(2,1)} custom-call(bf16[512,1024]{1,0:T(8,128)(2,1)} %q_hbm.1, bf16[512,1024]{1,0:T(8,128)(2,1)} %k_hbm.1, bf16[512,1024]{1,0:T(8,128)(2,1)} %v_hbm.1, f32[4096,1024]{1,0:T(8,128)} %taps_hbm.1, f32[1,1024]{1,0:T(1,128)} %bitcast.1, bf16[1024,4096]{1,0:T(8,128)(2,1)} %w_hbm.1, ...), custom_call_target="tpu_custom_call" | custom-call | flops 10000000000 | bytes 16777216 | tf_op jit(solution)/shard_map/pallas_call | solution.py:375
  73.7 2.3 %copy.10 = bf16[512,1024]{1,0:T(8,128)(2,1)} copy(bf16[512,1024]{1,0:T(8,128)(2,1)} %shard_map.82) | data formatting | bytes 2097152

commit v6 on v4

--- a/solution.py
+++ b/solution.py
@@ -73,7 +73,7 @@
 
 
 MESH = pl.DeviceIdType.MESH
-EIGHTHS = (2, 2, 2, 2)
+EIGHTHS = (1, 2, 2, 2, 1)
 AHEAD = 2
 ROWS = 8
 
@@ -365,6 +365,29 @@
             way_back(t, peer).wait_send()
 
 
+def hand_over_kernel(src_hbm, out_hbm, sems):
+    rows = src_hbm.shape[0] // 8
+    copies = []
+    for i in range(8):
+        piece = slice(i * rows, (i + 1) * rows)
+        copy = pltpu.make_async_copy(src_hbm.at[piece], out_hbm.at[piece], sems.at[i])
+        copy.start()
+        copies.append(copy)
+    for copy in copies:
+        copy.wait()
+
+
+def hand_over(result):
+    anywhere = pl.BlockSpec(memory_space=pl.ANY)
+    return pl.pallas_call(
+        hand_over_kernel,
+        out_shape=jax.ShapeDtypeStruct(result.shape, result.dtype),
+        in_specs=[anywhere],
+        out_specs=anywhere,
+        scratch_shapes=[pltpu.SemaphoreType.DMA((8,))],
+    )(result)
+
+
 def fused_body(forward, inverse, query_gate, key_gate, value_in, filter_taps, skip_gain, out_weight):
     length, width = query_gate.shape
     n = lax.axis_size("ctx")
@@ -372,7 +395,7 @@
     dma = pltpu.SemaphoreType.DMA
     anywhere = pl.BlockSpec(memory_space=pl.ANY)
     vmem = pl.BlockSpec(memory_space=pltpu.VMEM)
-    return pl.pallas_call(
+    result = pl.pallas_call(
         functools.partial(fused_kernel, n),
         out_shape=jax.ShapeDtypeStruct((length, width), BF16),
         in_specs=[anywhere] * 4 + [vmem] + [anywhere] * 3,
@@ -421,6 +444,7 @@
         query_gate, key_gate, value_in, filter_taps, skip_gain.reshape(1, width), out_weight,
         forward, inverse,
     )
+    return hand_over(result)
 
 
 def solution(mesh):

time: 72.3 us -> 108 us (1.49)
  Pallas kernels: 69.5 us -> 107 us
  local copies, waits for them, and re-layouts: 2.26 us -> 0 us
    pallas_call x0 -> x1, Pallas kernels: none -> 32.9 us  [hand_over(): pl.pallas_call(hand_over_kernel, out_shape=jax.ShapeDtypeStruct(result.sh...]
    pallas_call x1, Pallas kernels: 69.5 us -> 74.4 us  [fused_body(): pl.pallas_call(functools.partial(fused_kernel, n), out_shape=jax.ShapeDty...]
    unnamed x1 -> x0, local copies, waits for them, and re-layouts: 2.26 us -> none
where the time goes in v6:
time: 108 us
  Pallas kernels  107 us (99%)
    pallas_call x1, Pallas kernels, fused_body(): pl.pallas_call(functools.partial(fused_kernel, n), out_shape=jax.ShapeDty...  74.4 us
    pallas_call x1, Pallas kernels, hand_over(): pl.pallas_call(hand_over_kernel, out_shape=jax.ShapeDtypeStruct(result.sh...  32.9 us

profile of v6, /device:TPU:0, one launch (start us, length us, event | category | flops | bytes accessed | tf_op | source)
XLA Modules:
  0.0 107.6 jit_solution(14062700175463146011)
XLA Ops:
  0.0 74.4 %shard_map.82.src_hbm = bf16[512,1024]{1,0:T(8,128)(2,1)} custom-call(bf16[512,1024]{1,0:T(8,128)(2,1)} %q_hbm.1, bf16[512,1024]{1,0:T(8,128)(2,1)} %k_hbm.1, bf16[512,1024]{1,0:T(8,128)(2,1)} %v_hbm.1, f32[4096,1024]{1,0:T(8,128)} %taps_hbm.1, f32[1,1024]{1,0:T(1,128)} %bitcast.1, bf16[1024,4096]{1,0:T(8,128)(2,1)} %w_hbm.1, ...), custom_call_target="tpu_custom_call" | custom-call | flops 10000000000 | bytes 16777216 | tf_op jit(solution)/shard_map/pallas_call | solution.py:398
  74.5 32.9 %shard_map.83 = bf16[512,1024]{1,0:T(8,128)(2,1)} custom-call(bf16[512,1024]{1,0:T(8,128)(2,1)} %shard_map.82.src_hbm), custom_call_target="tpu_custom_call" | custom-call | tf_op jit(solution)/shard_map/pallas_call | solution.py:382

commit v7 on v4

--- a/solution.py
+++ b/solution.py
@@ -177,13 +177,6 @@
 
     taps_cols = pl.ds(pl.multiple_of(me * share, share), share)
     load_k, load_v = load(0, k_hbm, k_ref), load(1, v_hbm, v_ref)
-    load_fwd = load(2, fwd_hbm, fwd_ref)
-    load_taps = load(3, taps_hbm.at[:, taps_cols], taps_ref)
-    load_inv, load_q = load(4, inv_hbm, inv_ref), load(5, q_hbm, q_ref)
-    load_w = [
-        load(6 + i, w_hbm.at[:, pl.ds(pl.multiple_of(owner * width, width), width)], w_ref.at[i])
-        for i, owner in enumerate((opposite, beside, across, ch))
-    ]
 
     barrier = pltpu.get_barrier_semaphore()
     for peer in order:
@@ -193,6 +186,9 @@
 
     load_k.wait()
     load_v.wait()
+    load_fwd = load(2, fwd_hbm, fwd_ref)
+    load_taps = load(3, taps_hbm.at[:, taps_cols], taps_ref)
+    load_inv = load(4, inv_hbm, inv_ref)
     for d in range(n):
         cols = slice(d * share, (d + 1) * share)
         mixed[d] = (k_ref[:, cols].astype(F32) * v_ref[:, cols].astype(F32)).astype(BF16)
@@ -215,6 +211,11 @@
         sends.append(copy)
     own = pltpu.make_async_copy(mixed.at[me], recv1.at[me // 2, :, half(me)], own1_sem)
     own.start()
+    load_q = load(5, q_hbm, q_ref)
+    load_w = [
+        load(6 + i, w_hbm.at[:, pl.ds(pl.multiple_of(owner * width, width), width)], w_ref.at[i])
+        for i, owner in enumerate((opposite, beside, across, ch))
+    ]
 
     load_fwd.wait()
     load_taps.wait()

time: 72.3 us -> 72.4 us (level)
  no operation moved by 1% of the time
where the time goes in v7:
time: 72.4 us; the launch traced here: 71.7 us
  Pallas kernels  69.5 us (96%)
  local copies, waits for them, and re-layouts  2.26 us (3%)
    pallas_call x1, Pallas kernels, fused_body(): pl.pallas_call(functools.partial(fused_kernel, n), out_shape=jax.ShapeDty...  69.5 us
    unnamed x1, local copies, waits for them, and re-layouts  2.26 us

profile of v7, /device:TPU:0, one launch (start us, length us, event | category | flops | bytes accessed | tf_op | source)
XLA Modules:
  0.0 71.7 jit_solution(3186533489469646210)
XLA Ops:
  0.0 69.5 %shard_map.82 = bf16[512,1024]{1,0:T(8,128)(2,1)} custom-call(bf16[512,1024]{1,0:T(8,128)(2,1)} %q_hbm.1, bf16[512,1024]{1,0:T(8,128)(2,1)} %k_hbm.1, bf16[512,1024]{1,0:T(8,128)(2,1)} %v_hbm.1, f32[4096,1024]{1,0:T(8,128)} %taps_hbm.1, f32[1,1024]{1,0:T(1,128)} %bitcast.1, bf16[1024,4096]{1,0:T(8,128)(2,1)} %w_hbm.1, ...), custom_call_target="tpu_custom_call" | custom-call | flops 10000000000 | bytes 16777216 | tf_op jit(solution)/shard_map/pallas_call | solution.py:376
  69.5 2.3 %copy.10 = bf16[512,1024]{1,0:T(8,128)(2,1)} copy(bf16[512,1024]{1,0:T(8,128)(2,1)} %shard_map.82) | data formatting | bytes 2097152
